TPU v7x, 32 devices: a whole 2x2x4 slice. The times are simulated.
32 devices in a mesh: clips: 2 (over x), tile: 16 (over z, y, core).
Axes of the slice: x: 2, y: 2, z: 4, core: 2. Of those that a mesh axis runs over, the one named last changes fastest.
Arguments:
- latents: bfloat16 [12, 16, 8, 160], P('clips', 'tile'), parts along dimension 0, may hold values from -18 to 18
- w_in: bfloat16 [432, 384], replicated, may hold values from -0.3125 to 0.3125
- b_in: float32 [384], replicated, may hold values from -3 to 3
- gain_mid: float32 [384], replicated, may hold values from 0.1 to 1.9
- w_mid: bfloat16 [10368, 384], replicated, may hold values from -0.0625 to 0.0625
- b_mid: float32 [384], replicated, may hold values from -3 to 3
- w_up: bfloat16 [3456, 192], replicated, may hold values from -0.109375 to 0.109375
- b_up: float32 [192], replicated, may hold values from -3 to 3
Outputs:
- decoded: bfloat16 [8, 16, 16, 3840], P('clips', 'tile'), parts along dimension 0
There are 2 independent parts, one for each index of `clips`. A program takes and returns all parts, laid end to end along the dimension named above; an argument that names none is the same for every part. Nothing has to cross between parts.
All inputs are finite; a program needn't handle non-finite values.
Results may differ from a plain program's by a relative error of at most 0.006.
Values may be sent and summed in bfloat16 or wider, within the bound.
A program may use at most 128 MiB of HBM per device.

v0:
```python
import jax
import jax.numpy as jnp
from jax import lax
from jax.sharding import PartitionSpec as P

CACHE = 2
GC = 16


def passed_along(block, axis, distance):
    devices = range(lax.axis_size(axis))
    route = [(i - distance, i) for i in devices if i - distance in devices]
    return lax.ppermute(block, axis, route)


def pad_tile(field, width):
    position = lax.axis_index("tile")
    column = position % GC
    tile_cols = field.shape[2]
    tile_rows = field.shape[1]
    left_part = passed_along(field[:, :, tile_cols - width :, :], "tile", 1)
    right_part = passed_along(field[:, :, :width, :], "tile", -1)
    left_part = jnp.where(column == 0, jnp.zeros_like(left_part), left_part)
    right_part = jnp.where(column == GC - 1, jnp.zeros_like(right_part), right_part)
    widened = jnp.concatenate([left_part, field, right_part], axis=2)
    above_part = passed_along(widened[:, tile_rows - width :], "tile", GC)
    below_part = passed_along(widened[:, :width], "tile", -GC)
    return jnp.concatenate([above_part, widened, below_part], axis=1)


def causal_conv(padded, weight, out_rows, out_cols):
    frames = padded.shape[0]
    channels = padded.shape[3]
    out_chan = weight.shape[1]
    earlier = jnp.zeros((2,) + padded.shape[1:], padded.dtype)
    full = jnp.concatenate([earlier, padded], axis=0)
    if channels < 128:
        taps_list = [
            full[
                step_t : step_t + frames, step_y : step_y + out_rows, step_x : step_x + out_cols, :
            ]
            for step_t in range(3)
            for step_y in range(3)
            for step_x in range(3)
        ]
        patches = jnp.concatenate(taps_list, axis=-1).reshape(
            frames * out_rows * out_cols, 27 * channels
        )
        result = jnp.dot(patches, weight, preferred_element_type=jnp.float32)
        return result.reshape(frames, out_rows, out_cols, out_chan)
    total = jnp.zeros((frames * out_rows * out_cols, out_chan), jnp.float32)
    for step_y in range(3):
        for step_x in range(3):
            window = full[:, step_y : step_y + out_rows, step_x : step_x + out_cols, :].reshape(
                frames + 2, out_rows * out_cols, channels
            )
            for step_t in range(3):
                start = (9 * step_t + 3 * step_y + step_x) * channels
                taps = window[step_t : step_t + frames].reshape(
                    frames * out_rows * out_cols, channels
                )
                total = total + jnp.dot(
                    taps, weight[start : start + channels], preferred_element_type=jnp.float32
                )
    return total.reshape(frames, out_rows, out_cols, out_chan)


def activate(hidden, gain_mid):
    values = hidden.astype(jnp.float32)
    inverse = lax.rsqrt(jnp.mean(values * values, axis=-1, keepdims=True) + 1e-06)
    return jax.nn.silu(values * inverse * gain_mid).astype(jnp.bfloat16)


def upsample_conv(margin, w_up, b_up, tile_rows, tile_cols):
    out_frames = margin.shape[0]
    mid_chan = margin.shape[3]
    up_chan = w_up.shape[1]
    count = out_frames * tile_rows * tile_cols
    windows = {}
    for row_off in range(3):
        for col_off in range(3):
            windows[row_off, col_off] = margin[
                :, row_off : row_off + tile_rows, col_off : col_off + tile_cols, :
            ].reshape(count, mid_chan)
    phase_rows = []
    for phase_y in range(2):
        phase_cols = []
        for phase_x in range(2):
            total = jnp.zeros((count, up_chan), jnp.float32)
            for step_y in range(3):
                for step_x in range(3):
                    row_off = 1 + (phase_y + step_y - 1) // 2
                    col_off = 1 + (phase_x + step_x - 1) // 2
                    start = (3 * step_y + step_x) * mid_chan
                    total = total + jnp.dot(
                        windows[row_off, col_off],
                        w_up[start : start + mid_chan],
                        preferred_element_type=jnp.float32,
                    )
            phase_cols.append(
                (total + b_up)
                .astype(jnp.bfloat16)
                .reshape(out_frames, tile_rows, tile_cols, up_chan)
            )
        phase_rows.append(jnp.stack(phase_cols, axis=3))
    joined = jnp.stack(phase_rows, axis=2)
    return joined.reshape(out_frames, 1, 2 * tile_rows, 2 * tile_cols * up_chan)


def body(latents, w_in, b_in, gain_mid, w_mid, b_mid, w_up, b_up):
    frames = latents.shape[0]
    tile_rows = latents.shape[2]
    lat_chan = w_in.shape[0] // 27
    tile_cols = latents.shape[3] // lat_chan
    field = latents.reshape(frames, tile_rows, tile_cols, lat_chan)
    padded = pad_tile(field, 1)
    hidden = (causal_conv(padded, w_in, tile_rows, tile_cols) + b_in).astype(jnp.bfloat16)
    normed = pad_tile(activate(hidden, gain_mid), 1)
    residual = (
        hidden.astype(jnp.float32) + causal_conv(normed, w_mid, tile_rows, tile_cols) + b_mid
    ).astype(jnp.bfloat16)
    margin = pad_tile(residual[CACHE:], 1)
    return upsample_conv(margin, w_up, b_up, tile_rows, tile_cols)


def solution(mesh):
    placed = (P("clips", "tile", None, None), P(), P(), P(), P(), P(), P(), P())
    return jax.shard_map(
        body, mesh=mesh, in_specs=placed, out_specs=P("clips", "tile", None, None), check_vma=False
    )
```

profile of v0, /device:TPU:24, one launch (start us, length us, event | category | flops | bytes accessed | tf_op | source)
XLA Modules:
  0.0 153.2 jit_solution(17529338269801633642)
XLA Ops:
  1.0 2.8 %collective-permute-start.1 = (bf16[6,8,1,16]{3,2,1,0:T(2,128)(2,1)S(1)}, bf16[6,8,1,16]{3,2,1,0:T(2,128)(2,1)S(1)}, u32[]{:S(2)}, u32[]{:S(2)}) collective-permute-start(bf16[6,8,1,16]{3,2,1,0:T(2,128)(2,1)S(1)} %get-tuple-element.82), channel_id=1, source_target_pairs={{1,0},{2,1},{3,2},{4,3},{5,4},{6,5},{7,6},{8,7},{9,8},{10,9},{11,1... | collective-permute-start | bytes 4616 | tf_op jit(solution)/shard_map/ppermute | solution.py:13
  3.8 1.9 %collective-permute-start = (bf16[6,8,1,16]{3,2,1,0:T(2,128)(2,1)S(1)}, bf16[6,8,1,16]{3,2,1,0:T(2,128)(2,1)S(1)}, u32[]{:S(2)}, u32[]{:S(2)}) collective-permute-start(bf16[6,8,1,16]{3,2,1,0:T(2,128)(2,1)S(1)} %get-tuple-element.81), channel_id=1, source_target_pairs={{0,1},{1,2},{2,3},{3,4},{4,5},{5,6},{6,7},{7,8},{8,9},{9,10},{10,1... | collective-permute-start | bytes 4616 | tf_op jit(solution)/shard_map/ppermute | solution.py:13
  5.8 4.1 %collective-permute-done = bf16[6,8,1,16]{3,2,1,0:T(2,128)(2,1)S(1)} collective-permute-done((bf16[6,8,1,16]{3,2,1,0:T(2,128)(2,1)S(1)}, bf16[6,8,1,16]{3,2,1,0:T(2,128)(2,1)S(1)}, u32[]{:S(2)}, u32[]{:S(2)}) %collective-permute-start) | collective-permute-done | bytes 1568 | tf_op jit(solution)/shard_map/ppermute | solution.py:13
  12.4 1.5 fusion.123
  15.2 5.2 %concatenate.82 = bf16[6,8,10,432]{3,2,1,0:T(8,128)(2,1)} concatenate(bf16[6,8,10,16]{3,2,1,0:T(8,128)(2,1)} %get-tuple-element.68, bf16[6,8,10,16]{3,2,1,0:T(8,128)(2,1)} %get-tuple-element.67, bf16[6,8,10,16]{3,2,1,0:T(8,128)(2,1)} %get-tuple-element.66, bf16[6,8,10,16]{3,2,1,0:T(8,128)(2,1)S(1)} %get-tuple-element.65, bf16[6,8,10,16]{3,2,1,0:T(8,128)(2,1)S(1)} %get-tuple-element.64, ...), dimensions={3} | concatenate | bytes 829440 | tf_op jit(solution)/shard_map/concatenate | solution.py:46
  20.4 1.8 %fusion.6 = (f32[6,8,10]{2,1,0:T(8,128)S(1)}, bf16[6,8,10,384]{3,2,1,0:T(8,128)(2,1)S(1)}) fusion(f32[384]{0:T(512)S(1)} %copy-done.51, bf16[6,8,10,432]{3,2,1,0:T(8,128)(2,1)} %concatenate.82, bf16[432,384]{1,0:T(8,128)(2,1)S(1)} %copy-done), kind=kOutput, calls=%fused_computation.37 | convolution fusion | flops 160173600 | bytes 1118592 | tf_op jit(solution)/shard_map/dot_general | solution.py:49
  22.8 1.9 %collective-permute-start.5 = (bf16[6,8,1,384]{3,2,1,0:T(2,128)(2,1)S(1)}, bf16[6,8,1,384]{3,2,1,0:T(2,128)(2,1)S(1)}, u32[]{:S(2)}, u32[]{:S(2)}) collective-permute-start(bf16[6,8,1,384]{3,2,1,0:T(2,128)(2,1)S(1)} %get-tuple-element.38), channel_id=1, source_target_pairs={{1,0},{2,1},{3,2},{4,3},{5,4},{6,5},{7,6},{8,7},{9,8},{10,9},{11,1... | collective-permute-start | bytes 110600 | tf_op jit(solution)/shard_map/ppermute | solution.py:13
  25.6 2.4 %collective-permute-start.4 = (bf16[6,8,1,384]{3,2,1,0:T(2,128)(2,1)S(1)}, bf16[6,8,1,384]{3,2,1,0:T(2,128)(2,1)S(1)}, u32[]{:S(2)}, u32[]{:S(2)}) collective-permute-start(bf16[6,8,1,384]{3,2,1,0:T(2,128)(2,1)S(1)} %get-tuple-element.37), channel_id=1, source_target_pairs={{0,1},{1,2},{2,3},{3,4},{4,5},{5,6},{6,7},{7,8},{8,9},{9,10},{10,1... | collective-permute-start | bytes 110600 | tf_op jit(solution)/shard_map/ppermute | solution.py:13
  28.1 4.1 %collective-permute-done.4 = bf16[6,8,1,384]{3,2,1,0:T(2,128)(2,1)S(1)} collective-permute-done((bf16[6,8,1,384]{3,2,1,0:T(2,128)(2,1)S(1)}, bf16[6,8,1,384]{3,2,1,0:T(2,128)(2,1)S(1)}, u32[]{:S(2)}, u32[]{:S(2)}) %collective-permute-start.4) | collective-permute-done | bytes 36896 | tf_op jit(solution)/shard_map/ppermute | solution.py:13
  36.4 4.2 %fusion.116 = (bf16[6,8,10,384]{3,2,1,0:T(8,128)(2,1)}, bf16[6,8,10,384]{3,2,1,0:T(8,128)(2,1)}, bf16[6,8,10,384]{3,2,1,0:T(8,128)(2,1)}, bf16[6,8,10,384]{3,2,1...) fusion(bf16[8,10,12,384]{3,2,1,0:T(8,128)(2,1)S(1)} %fusion.41), kind=kLoop, calls=%fused_computation.195 | loop fusion | bytes 13271040 | tf_op jit(solution)/shard_map/slice | solution.py:59
  44.3 2.0 %reshape.281 = bf16[480,384]{1,0:T(8,128)(2,1)} reshape(bf16[6,8,10,384]{3,2,1,0:T(8,128)(2,1)} %get-tuple-element.20) | data formatting | bytes 737280 | tf_op jit(solution)/shard_map/reshape | solution.py:59
  46.4 1.9 %reshape.282 = bf16[480,384]{1,0:T(8,128)(2,1)} reshape(bf16[6,8,10,384]{3,2,1,0:T(8,128)(2,1)} %get-tuple-element.19) | data formatting | bytes 737280 | tf_op jit(solution)/shard_map/reshape | solution.py:59
  50.1 2.0 %reshape.285 = bf16[480,384]{1,0:T(8,128)(2,1)} reshape(bf16[6,8,10,384]{3,2,1,0:T(8,128)(2,1)} %get-tuple-element.17) | data formatting | bytes 737280 | tf_op jit(solution)/shard_map/reshape | solution.py:59
  53.1 2.0 %reshape.287 = bf16[480,384]{1,0:T(8,128)(2,1)} reshape(bf16[6,8,10,384]{3,2,1,0:T(8,128)(2,1)} %get-tuple-element.16) | data formatting | bytes 737280 | tf_op jit(solution)/shard_map/reshape | solution.py:59
  57.7 2.0 %reshape.293 = bf16[480,384]{1,0:T(8,128)(2,1)} reshape(bf16[6,8,10,384]{3,2,1,0:T(8,128)(2,1)} %get-tuple-element.12) | data formatting | bytes 737280 | tf_op jit(solution)/shard_map/reshape | solution.py:59
  63.7 2.0 %reshape.299 = bf16[480,384]{1,0:T(8,128)(2,1)} reshape(bf16[6,8,10,384]{3,2,1,0:T(8,128)(2,1)} %get-tuple-element.8) | data formatting | bytes 737280 | tf_op jit(solution)/shard_map/reshape | solution.py:59
  65.7 2.0 %reshape.300 = bf16[480,384]{1,0:T(8,128)(2,1)} reshape(bf16[6,8,10,384]{3,2,1,0:T(8,128)(2,1)} %get-tuple-element.7) | data formatting | bytes 737280 | tf_op jit(solution)/shard_map/reshape | solution.py:59
  69.0 1.5 fusion.80
  70.5 1.6 %convolution_add_fusion.26 = f32[480,384]{1,0:T(8,128)S(1)} fusion(f32[480,384]{1,0:T(8,128)S(1)} %fusion.80, bf16[480,384]{1,0:T(8,128)(2,1)} %reshape.279, bf16[10368,384]{1,0:T(8,128)(2,1)} %param.12), kind=kOutput, calls=%fused_computation.36 | convolution fusion | flops 141742080 | bytes 2138112 | tf_op jit(solution)/shard_map/dot_general | solution.py:62
  72.1 1.3 convolution_add_fusion.25
  73.5 1.4 convolution_add_fusion.24
  75.0 1.5 convolution_add_fusion.23
  76.5 1.4 convolution_add_fusion.22
  77.9 1.4 convolution_add_fusion.21
  79.3 1.4 convolution_add_fusion.20
  100.5 1.9 %collective-permute-start.9 = (bf16[4,8,1,384]{3,2,1,0:T(2,128)(2,1)S(1)}, bf16[4,8,1,384]{3,2,1,0:T(2,128)(2,1)S(1)}, u32[]{:S(2)}, u32[]{:S(2)}) collective-permute-start(bf16[4,8,1,384]{3,2,1,0:T(2,128)(2,1)S(1)} %get-tuple-element.34), channel_id=1, source_target_pairs={{1,0},{2,1},{3,2},{4,3},{5,4},{6,5},{7,6},{8,7},{9,8},{10,9},{11,1... | collective-permute-start | bytes 73736 | tf_op jit(solution)/shard_map/ppermute | solution.py:13
  104.3 2.4 %collective-permute-start.8 = (bf16[4,8,1,384]{3,2,1,0:T(2,128)(2,1)S(1)}, bf16[4,8,1,384]{3,2,1,0:T(2,128)(2,1)S(1)}, u32[]{:S(2)}, u32[]{:S(2)}) collective-permute-start(bf16[4,8,1,384]{3,2,1,0:T(2,128)(2,1)S(1)} %get-tuple-element.33), channel_id=1, source_target_pairs={{0,1},{1,2},{2,3},{3,4},{4,5},{5,6},{6,7},{7,8},{8,9},{9,10},{10,1... | collective-permute-start | bytes 73736 | tf_op jit(solution)/shard_map/ppermute | solution.py:13
  106.8 3.8 %collective-permute-done.8 = bf16[4,8,1,384]{3,2,1,0:T(2,128)(2,1)S(1)} collective-permute-done((bf16[4,8,1,384]{3,2,1,0:T(2,128)(2,1)S(1)}, bf16[4,8,1,384]{3,2,1,0:T(2,128)(2,1)S(1)}, u32[]{:S(2)}, u32[]{:S(2)}) %collective-permute-start.8) | collective-permute-done | bytes 24608 | tf_op jit(solution)/shard_map/ppermute | solution.py:13
  111.4 1.3 pad_maximum_fusion.6
  112.7 1.1 reshape.308
  114.7 1.9 %convolution_add_fusion.34 = f32[320,192]{0,1:T(8,128)} fusion(f32[320,192]{0,1:T(8,128)} %copy-done.12, bf16[320,384]{1,0:T(8,128)(2,1)S(1)} %reshape.308, bf16[3456,192]{0,1:T(8,128)(2,1)S(1)} %copy-done.2), kind=kOutput, calls=%fused_computation.60 | convolution fusion | flops 47247360 | bytes 884736 | tf_op jit(solution)/shard_map/dot_general | solution.py:95
  117.3 1.3 collective-permute-start.11
  118.6 1.1 reshape.311
  120.0 2.1 %fusion.32 = f32[320,192]{0,1:T(8,128)} fusion(f32[320,192]{0,1:T(8,128)S(1)} %fusion.88, f32[320,192]{0,1:T(8,128)S(1)} %fusion.82, f32[320,192]{0,1:T(8,128)S(1)} %fusion.92, f32[320,192]{0,1:T(8,128)} %convolution_add_fusion.30, bf16[320,384]{1,0:T(8,128)(2,1)S(1)} %reshape.311, bf16[3456,192]{0,1:T(8,128)(2,1)S(1)} %copy-done.2), kind=kOutput, calls=%fused_computation.79 | convolution fusion | flops 47431680 | bytes 1769472 | tf_op jit(solution)/shard_map/dot_general | solution.py:95
  123.1 1.2 maximum_maximum_fusion.1
  124.3 1.1 fusion.122
  125.5 1.1 reshape.313
  127.5 1.1 reshape.314
  128.6 1.3 fusion.17
  132.0 1.8 %reshape.312 = bf16[320,384]{1,0:T(8,128)(2,1)} reshape(bf16[4,8,10,384]{3,2,1,0:T(8,128)(2,1)} %get-tuple-element.46) | data formatting | bytes 491520 | tf_op jit(solution)/shard_map/reshape | solution.py:84
  133.8 1.4 fusion.20
  136.4 1.1 fusion.121
  137.5 1.1 reshape.307
  140.6 1.8 %reshape.310 = bf16[320,384]{1,0:T(8,128)(2,1)} reshape(bf16[4,8,10,384]{3,2,1,0:T(8,128)(2,1)} %get-tuple-element.44) | data formatting | bytes 491520 | tf_op jit(solution)/shard_map/reshape | solution.py:84
  142.4 1.5 fusion.34
  145.1 1.1 copy.15
  148.1 1.3 convolution_add_fusion.42
  152.0 1.2 reshape.315
  (221 shorter events, 61.8 us)
Async XLA Ops:
  0.0 20.4 %copy-start = (bf16[432,384]{1,0:T(8,128)(2,1)S(1)}, bf16[432,384]{1,0:T(8,128)(2,1)}, u32[]{:S(2)}) copy-start(bf16[432,384]{1,0:T(8,128)(2,1)} %param.9) | copy-start | bytes 995332
  1.0 4.7 %collective-permute-start.1 = (bf16[6,8,1,16]{3,2,1,0:T(2,128)(2,1)S(1)}, bf16[6,8,1,16]{3,2,1,0:T(2,128)(2,1)S(1)}, u32[]{:S(2)}, u32[]{:S(2)}) collective-permute-start(bf16[6,8,1,16]{3,2,1,0:T(2,128)(2,1)S(1)} %get-tuple-element.82), channel_id=1, source_target_pairs={{1,0},{2,1},{3,2},{4,3},{5,4},{6,5},{7,6},{8,7},{9,8},{10,9},{11,1... | collective-permute-start | bytes 4616 | tf_op jit(solution)/shard_map/ppermute | solution.py:13
  3.8 6.0 %collective-permute-start = (bf16[6,8,1,16]{3,2,1,0:T(2,128)(2,1)S(1)}, bf16[6,8,1,16]{3,2,1,0:T(2,128)(2,1)S(1)}, u32[]{:S(2)}, u32[]{:S(2)}) collective-permute-start(bf16[6,8,1,16]{3,2,1,0:T(2,128)(2,1)S(1)} %get-tuple-element.81), channel_id=1, source_target_pairs={{0,1},{1,2},{2,3},{3,4},{4,5},{5,6},{6,7},{7,8},{8,9},{9,10},{10,1... | collective-permute-start | bytes 4616 | tf_op jit(solution)/shard_map/ppermute | solution.py:13
  9.9 2.3 %collective-permute-start.3 = (bf16[6,1,12,16]{3,2,1,0:T(8,128)(2,1)S(1)}, bf16[6,1,12,16]{3,2,1,0:T(8,128)(2,1)S(1)}, u32[]{:S(2)}, u32[]{:S(2)}) collective-permute-start(bf16[6,1,12,16]{3,2,1,0:T(8,128)(2,1)S(1)} %get-tuple-element.72), channel_id=1, source_target_pairs={} | collective-permute-start | bytes 6920 | tf_op jit(solution)/shard_map/ppermute | solution.py:13
  10.6 1.6 %collective-permute-start.2 = (bf16[6,1,12,16]{3,2,1,0:T(8,128)(2,1)S(1)}, bf16[6,1,12,16]{3,2,1,0:T(8,128)(2,1)S(1)}, u32[]{:S(2)}, u32[]{:S(2)}) collective-permute-start(bf16[6,1,12,16]{3,2,1,0:T(8,128)(2,1)S(1)} %get-tuple-element.71), channel_id=1, source_target_pairs={} | collective-permute-start | bytes 6920 | tf_op jit(solution)/shard_map/ppermute | solution.py:13
  15.2 5.2 %copy-start.51 = (f32[384]{0:T(512)S(1)}, f32[384]{0:T(512)}, u32[]{:S(2)}) copy-start(f32[384]{0:T(512)} %param.10) | copy-start | bytes 4612
  20.4 1.8 %copy-start.49 = (f32[384]{0:T(512)S(1)}, f32[384]{0:T(512)}, u32[]{:S(2)}) copy-start(f32[384]{0:T(512)} %param.11) | copy-start | bytes 4612
  22.8 5.2 %collective-permute-start.5 = (bf16[6,8,1,384]{3,2,1,0:T(2,128)(2,1)S(1)}, bf16[6,8,1,384]{3,2,1,0:T(2,128)(2,1)S(1)}, u32[]{:S(2)}, u32[]{:S(2)}) collective-permute-start(bf16[6,8,1,384]{3,2,1,0:T(2,128)(2,1)S(1)} %get-tuple-element.38), channel_id=1, source_target_pairs={{1,0},{2,1},{3,2},{4,3},{5,4},{6,5},{7,6},{8,7},{9,8},{10,9},{11,1... | collective-permute-start | bytes 110600 | tf_op jit(solution)/shard_map/ppermute | solution.py:13
  25.6 6.6 %collective-permute-start.4 = (bf16[6,8,1,384]{3,2,1,0:T(2,128)(2,1)S(1)}, bf16[6,8,1,384]{3,2,1,0:T(2,128)(2,1)S(1)}, u32[]{:S(2)}, u32[]{:S(2)}) collective-permute-start(bf16[6,8,1,384]{3,2,1,0:T(2,128)(2,1)S(1)} %get-tuple-element.37), channel_id=1, source_target_pairs={{0,1},{1,2},{2,3},{3,4},{4,5},{5,6},{6,7},{7,8},{8,9},{9,10},{10,1... | collective-permute-start | bytes 110600 | tf_op jit(solution)/shard_map/ppermute | solution.py:13
  32.3 3.7 %collective-permute-start.7 = (bf16[6,1,12,384]{3,2,1,0:T(8,128)(2,1)S(1)}, bf16[6,1,12,384]{3,2,1,0:T(8,128)(2,1)S(1)}, u32[]{:S(2)}, u32[]{:S(2)}) collective-permute-start(bf16[6,1,12,384]{3,2,1,0:T(8,128)(2,1)S(1)} %get-tuple-element.26), channel_id=1, source_target_pairs={} | collective-permute-start | bytes 165896 | tf_op jit(solution)/shard_map/ppermute | solution.py:13
  33.0 3.0 %collective-permute-start.6 = (bf16[6,1,12,384]{3,2,1,0:T(8,128)(2,1)S(1)}, bf16[6,1,12,384]{3,2,1,0:T(8,128)(2,1)S(1)}, u32[]{:S(2)}, u32[]{:S(2)}) collective-permute-start(bf16[6,1,12,384]{3,2,1,0:T(8,128)(2,1)S(1)} %get-tuple-element.25), channel_id=1, source_target_pairs={} | collective-permute-start | bytes 165896 | tf_op jit(solution)/shard_map/ppermute | solution.py:13
  44.3 4.8 %copy-start.22 = (bf16[6,8,10,384]{3,2,1,0:T(8,128)(2,1)S(1)}, bf16[6,8,10,384]{3,2,1,0:T(8,128)(2,1)}, u32[]{:S(2)}) copy-start(bf16[6,8,10,384]{3,2,1,0:T(8,128)(2,1)} %get-tuple-element.18) | copy-start | bytes 1105924
  50.1 5.0 %copy-start.21 = (bf16[6,8,10,384]{3,2,1,0:T(8,128)(2,1)S(1)}, bf16[6,8,10,384]{3,2,1,0:T(8,128)(2,1)}, u32[]{:S(2)}) copy-start(bf16[6,8,10,384]{3,2,1,0:T(8,128)(2,1)} %get-tuple-element.15) | copy-start | bytes 1105924
  52.1 3.8 %copy-start.20 = (bf16[6,8,10,384]{3,2,1,0:T(8,128)(2,1)S(1)}, bf16[6,8,10,384]{3,2,1,0:T(8,128)(2,1)}, u32[]{:S(2)}) copy-start(bf16[6,8,10,384]{3,2,1,0:T(8,128)(2,1)} %get-tuple-element.14) | copy-start | bytes 1105924
  53.1 3.8 %copy-start.19 = (bf16[6,8,10,384]{3,2,1,0:T(8,128)(2,1)S(1)}, bf16[6,8,10,384]{3,2,1,0:T(8,128)(2,1)}, u32[]{:S(2)}) copy-start(bf16[6,8,10,384]{3,2,1,0:T(8,128)(2,1)} %get-tuple-element.13) | copy-start | bytes 1105924
  56.0 3.8 %copy-start.18 = (bf16[6,8,10,384]{3,2,1,0:T(8,128)(2,1)S(1)}, bf16[6,8,10,384]{3,2,1,0:T(8,128)(2,1)}, u32[]{:S(2)}) copy-start(bf16[6,8,10,384]{3,2,1,0:T(8,128)(2,1)} %get-tuple-element.11) | copy-start | bytes 1105924
  56.8 3.8 %copy-start.17 = (bf16[6,8,10,384]{3,2,1,0:T(8,128)(2,1)S(1)}, bf16[6,8,10,384]{3,2,1,0:T(8,128)(2,1)}, u32[]{:S(2)}) copy-start(bf16[6,8,10,384]{3,2,1,0:T(8,128)(2,1)} %get-tuple-element.10) | copy-start | bytes 1105924
  57.7 3.8 %copy-start.16 = (bf16[6,8,10,384]{3,2,1,0:T(8,128)(2,1)S(1)}, bf16[6,8,10,384]{3,2,1,0:T(8,128)(2,1)}, u32[]{:S(2)}) copy-start(bf16[6,8,10,384]{3,2,1,0:T(8,128)(2,1)} %get-tuple-element.9) | copy-start | bytes 1105924
  63.7 4.9 %copy-start.15 = (bf16[6,8,10,384]{3,2,1,0:T(8,128)(2,1)S(1)}, bf16[6,8,10,384]{3,2,1,0:T(8,128)(2,1)}, u32[]{:S(2)}) copy-start(bf16[6,8,10,384]{3,2,1,0:T(8,128)(2,1)} %get-tuple-element.6) | copy-start | bytes 1105924
  65.7 3.0 %copy-start.14 = (bf16[6,8,10,384]{3,2,1,0:T(8,128)(2,1)S(1)}, bf16[6,8,10,384]{3,2,1,0:T(8,128)(2,1)}, u32[]{:S(2)}) copy-start(bf16[6,8,10,384]{3,2,1,0:T(8,128)(2,1)} %get-tuple-element.5) | copy-start | bytes 1105924
  69.0 3.2 %copy-start.44 = (bf16[480,384]{1,0:T(8,128)(2,1)S(1)}, bf16[480,384]{1,0:T(8,128)(2,1)}, u32[]{:S(2)}) copy-start(bf16[480,384]{1,0:T(8,128)(2,1)} %reshape.280) | copy-start | bytes 1105924
  69.0 4.5 %copy-start.43 = (bf16[480,384]{1,0:T(8,128)(2,1)S(1)}, bf16[480,384]{1,0:T(8,128)(2,1)}, u32[]{:S(2)}) copy-start(bf16[480,384]{1,0:T(8,128)(2,1)} %reshape.281) | copy-start | bytes 1105924
  70.5 10.2 %slice-start = ((s8[7962624]{0:T(1024)(128)(4,1)}), s8[4194304]{0:T(1024)(128)(4,1)S(1)}, s32[]{:S(2)}) async-start(s8[7962624]{0:T(1024)(128)(4,1)} %bitcast.67), calls=%async_computation | async-start | bytes 8388608
  73.5 1.4 copy-start.42
  73.5 2.9 %copy-start.41 = (bf16[480,384]{1,0:T(8,128)(2,1)S(1)}, bf16[480,384]{1,0:T(8,128)(2,1)}, u32[]{:S(2)}) copy-start(bf16[480,384]{1,0:T(8,128)(2,1)} %reshape.283) | copy-start | bytes 1105924
  74.9 5.8 %slice-start.1 = ((s8[7962624]{0:T(1024)(128)(4,1)}), s8[3768320]{0:T(1024)(128)(4,1)S(1)}, s32[]{:S(2)}) async-start(s8[7962624]{0:T(1024)(128)(4,1)} %bitcast.67), calls=%async_computation.1 | async-start | bytes 7536640
  76.5 1.4 copy-start.40
  77.9 1.4 copy-start.38
  79.3 1.4 copy-start.39
  80.8 1.0 copy-start.37
  98.0 1.3 copy-start.2
  99.9 20.1 %copy-start.7 = (f32[320,192]{0,1:T(8,128)}, f32[320,192]{0,1:T(8,128)S(1)}, u32[]{:S(2)}) copy-start(f32[320,192]{0,1:T(8,128)S(1)} %fusion.92) | copy-start | bytes 737284
  100.2 11.2 %copy-start.12 = (f32[320,192]{0,1:T(8,128)}, f32[320,192]{0,1:T(8,128)S(1)}, u32[]{:S(2)}) copy-start(f32[320,192]{0,1:T(8,128)S(1)} %fusion.96) | copy-start | bytes 737284
  100.4 21.6 %copy-start.3 = (f32[320,192]{0,1:T(8,128)}, f32[320,192]{0,1:T(8,128)S(1)}, u32[]{:S(2)}) copy-start(f32[320,192]{0,1:T(8,128)S(1)} %fusion.90) | copy-start | bytes 737284
  100.5 6.3 %collective-permute-start.9 = (bf16[4,8,1,384]{3,2,1,0:T(2,128)(2,1)S(1)}, bf16[4,8,1,384]{3,2,1,0:T(2,128)(2,1)S(1)}, u32[]{:S(2)}, u32[]{:S(2)}) collective-permute-start(bf16[4,8,1,384]{3,2,1,0:T(2,128)(2,1)S(1)} %get-tuple-element.34), channel_id=1, source_target_pairs={{1,0},{2,1},{3,2},{4,3},{5,4},{6,5},{7,6},{8,7},{9,8},{10,9},{11,1... | collective-permute-start | bytes 73736 | tf_op jit(solution)/shard_map/ppermute | solution.py:13
  104.3 6.3 %collective-permute-start.8 = (bf16[4,8,1,384]{3,2,1,0:T(2,128)(2,1)S(1)}, bf16[4,8,1,384]{3,2,1,0:T(2,128)(2,1)S(1)}, u32[]{:S(2)}, u32[]{:S(2)}) collective-permute-start(bf16[4,8,1,384]{3,2,1,0:T(2,128)(2,1)S(1)} %get-tuple-element.33), channel_id=1, source_target_pairs={{0,1},{1,2},{2,3},{3,4},{4,5},{5,6},{6,7},{7,8},{8,9},{9,10},{10,1... | collective-permute-start | bytes 73736 | tf_op jit(solution)/shard_map/ppermute | solution.py:13
  116.7 6.4 %collective-permute-start.10 = (bf16[4,1,12,384]{3,2,1,0:T(8,128)(2,1)}, bf16[4,1,12,384]{3,2,1,0:T(8,128)(2,1)S(1)}, u32[]{:S(2)}, u32[]{:S(2)}) collective-permute-start(bf16[4,1,12,384]{3,2,1,0:T(8,128)(2,1)} %get-tuple-element.41), channel_id=1, source_target_pairs={} | collective-permute-start | bytes 110600 | tf_op jit(solution)/shard_map/ppermute | solution.py:13
  117.3 5.8 %collective-permute-start.11 = (bf16[4,1,12,384]{3,2,1,0:T(8,128)(2,1)}, bf16[4,1,12,384]{3,2,1,0:T(8,128)(2,1)}, u32[]{:S(2)}, u32[]{:S(2)}) collective-permute-start(bf16[4,1,12,384]{3,2,1,0:T(8,128)(2,1)} %get-tuple-element.42), channel_id=1, source_target_pairs={} | collective-permute-start | bytes 110600 | tf_op jit(solution)/shard_map/ppermute | solution.py:13
  119.7 2.4 %copy-start.9 = (f32[320,192]{0,1:T(8,128)S(1)}, f32[320,192]{0,1:T(8,128)}, u32[]{:S(2)}) copy-start(f32[320,192]{0,1:T(8,128)} %fusion.94) | copy-start | bytes 737284
  119.7 2.4 %copy-start.45 = (f32[320,192]{0,1:T(8,128)S(1)}, f32[320,192]{0,1:T(8,128)}, u32[]{:S(2)}) copy-start(f32[320,192]{0,1:T(8,128)} %convolution_add_fusion.34) | copy-start | bytes 737284
  120.0 3.1 %copy-start.11 = (f32[320,192]{0,1:T(8,128)}, f32[320,192]{0,1:T(8,128)S(1)}, u32[]{:S(2)}) copy-start(f32[320,192]{0,1:T(8,128)S(1)} %fusion.88) | copy-start | bytes 737284
  126.5 3.4 %copy-start.48 = (f32[192]{0:T(256)S(1)}, f32[192]{0:T(256)}, u32[]{:S(2)}) copy-start(f32[192]{0:T(256)} %param.15) | copy-start | bytes 2308
  137.5 4.9 %copy-start.8 = (f32[320,192]{0,1:T(8,128)S(1)}, f32[320,192]{0,1:T(8,128)}, u32[]{:S(2)}) copy-start(f32[320,192]{0,1:T(8,128)} %copy-done.7) | copy-start | bytes 737284
  140.6 3.3 %copy-start.5 = (f32[320,192]{0,1:T(8,128)S(1)}, f32[320,192]{0,1:T(8,128)}, u32[]{:S(2)}) copy-start(f32[320,192]{0,1:T(8,128)} %fusion.86) | copy-start | bytes 737284
  145.1 4.2 %copy-start.4 = (f32[320,192]{0,1:T(8,128)S(1)}, f32[320,192]{0,1:T(8,128)}, u32[]{:S(2)}) copy-start(f32[320,192]{0,1:T(8,128)} %copy-done.3) | copy-start | bytes 737284
  145.1 4.3 %copy-start.10 = (f32[320,192]{0,1:T(8,128)S(1)}, f32[320,192]{0,1:T(8,128)}, u32[]{:S(2)}) copy-start(f32[320,192]{0,1:T(8,128)} %fusion.94) | copy-start | bytes 737284
  148.1 1.6 %copy-start.6 = (f32[320,192]{0,1:T(8,128)S(1)}, f32[320,192]{0,1:T(8,128)}, u32[]{:S(2)}) copy-start(f32[320,192]{0,1:T(8,128)} %fusion.86) | copy-start | bytes 737284
  151.1 2.1 %copy-start.1 = (bf16[432,384]{1,0:T(8,128)(2,1)S(1)}, bf16[432,384]{1,0:T(8,128)(2,1)}, u32[]{:S(2)}) copy-start(bf16[432,384]{1,0:T(8,128)(2,1)} %param.9) | copy-start | bytes 995332
  (18 other events, 17.2 us)
where the time goes:
time: 155 us; the launch traced here: 153 us
  local copies, waits for them, and re-layouts  74.2 us (48%)
  matrix products  40.2 us (26%)
  starting transfers between devices  17.8 us (11%)
  waiting for transfers between devices  11.9 us (8%)
  other arithmetic  7.9 us (5%)
    reshape x27, local copies, waits for them, and re-layouts, causal_conv(): window[step_t:step_t + frames]  29.4 us
    dot_general x25, matrix products, upsample_conv(): jnp.dot(windows[row_off, col_off], w_up[start:start + mid_chan], preferre...  19.5 us
    dot_general x27, matrix products, causal_conv(): jnp.dot(taps, weight[start:start + channels], preferred_element_type=jnp....  19 us
    ppermute x12, starting transfers between devices, passed_along(): return lax.ppermute(block, axis, route)  17.8 us
    ppermute x12, waiting for transfers between devices, passed_along(): return lax.ppermute(block, axis, route)  11.9 us
    unnamed x108, local copies, waits for them, and re-layouts  11.7 us
    reshape x9, local copies, waits for them, and re-layouts, upsample_conv(): windows[row_off, col_off] = margin[:, row_off:row_off + tile_rows, col_of...  10.3 us
    concatenate x1, local copies, waits for them, and re-layouts, causal_conv(): jnp.concatenate(taps_list, axis=-1)  5.18 us
  transfers between devices with their start and end apart: 12, of which 3 were waited for; matrix products, arithmetic and copies ran while one was open for 7% of the time, Pallas kernels for 0%

commit v1 on v0

v1 whole, which is shorter than its diff:
```python
import functools

import jax
import jax.numpy as jnp
from jax import lax
from jax.experimental import pallas as pl
from jax.experimental.pallas import tpu as pltpu
from jax.sharding import PartitionSpec as P

CACHE = 2
GC = 16
BF = jnp.bfloat16
F32 = jnp.float32
MESH = pl.DeviceIdType.MESH


def shift_rows(v, b):
    if b == 1:
        return v
    rows = v.shape[1]
    row = lax.broadcasted_iota(jnp.int32, v.shape, 1)
    moved = pltpu.roll(v, 1 if b == 0 else rows - 1, 1)
    return jnp.where(row == (0 if b == 0 else rows - 1), 0.0, moved)


def kernel(
    sizes, lat, w_in, b_in, gain, w_mid, b_mid, w_up, b_up, out,
    xin, xrecv, xs, win_v, wpad, wmid_v, wup_v, wc, bias, lhs, hacc, hbuf, nab, acc, rb, outs,
    send_sem, recv_sem, in_sem, up_sem, mid_sem,
):
    frames, th, tw, cl, cm, cu, gr, rows, off = sizes
    keep = frames - CACHE
    nw, rw = tw + 4, tw + 2
    me = lax.axis_index("tile")
    col, grow = lax.rem(me, GC), lax.div(me, GC)

    in_copy = pltpu.make_async_copy(w_in, win_v, in_sem)
    up_copy = pltpu.make_async_copy(w_up, wup_v, up_sem)
    part = 9 * cm
    mid_copies = [
        pltpu.make_async_copy(
            w_mid.at[pl.ds(a * part, part), :], wmid_v.at[pl.ds(a * part, part), :], mid_sem.at[a]
        )
        for a in range(3)
    ]

    steps = [(0, -1), (0, 1)]
    if gr > 1:
        steps += [(-1, -1), (-1, 0), (-1, 1), (1, -1), (1, 0), (1, 1)]

    def there(step):
        dr, dc = step
        ok = (col + dc >= 0) & (col + dc < GC)
        if dr:
            ok = ok & (grow + dr >= 0) & (grow + dr < gr)
        return ok

    barrier = pltpu.get_barrier_semaphore()
    for step in steps:
        @pl.when(there(step))
        def _():
            pl.semaphore_signal(
                barrier, inc=1, device_id={"tile": me + step[0] * GC + step[1]}, device_id_type=MESH
            )

    in_copy.start()
    up_copy.start()
    for copy in mid_copies:
        copy.start()

    xin[...] = jnp.zeros_like(xin)
    xin[:, 0 : tw * cl] = lat[...]
    for k, step in enumerate(steps):
        @pl.when(jnp.logical_not(there(step)))
        def _():
            xrecv[k] = jnp.zeros(xin.shape, BF)

    pl.semaphore_wait(barrier, sum(there(step).astype(jnp.int32) for step in steps))

    def copy_to(k, slot):
        dr, dc = steps[k]
        return pltpu.make_async_remote_copy(
            src_ref=xin,
            dst_ref=xrecv.at[slot],
            send_sem=send_sem.at[k],
            recv_sem=recv_sem.at[slot],
            device_id={"tile": me + dr * GC + dc},
            device_id_type=MESH,
        )

    for k, (dr, dc) in enumerate(steps):
        @pl.when(there((dr, dc)))
        def _():
            copy_to(k, steps.index((-dr, -dc))).start()

    wpad[...] = jnp.zeros_like(wpad)
    in_copy.wait()
    for g in range(9):
        wpad[g * 128 : g * 128 + 3 * cl, :] = win_v[g * 3 * cl : (g + 1) * 3 * cl, :]

    wide = 2 * cu - 128
    bias[...] = jnp.zeros_like(bias)
    bias[0:1, 0:cu] = b_up[...].reshape(1, cu)
    first = bias[...]
    second = pltpu.roll(first, wide - cu, 1)
    bias3 = jnp.concatenate(
        [first[0:1, :128], first[0:1, 128:] + second[0:1, :128], second[0:1, 128:]], axis=1
    )

    up_copy.wait()
    blk = 16
    for phase in range(4):
        spare = pl.ds(0, wide - cu) if phase % 2 else pl.ds(cu, wide - cu)
        wc[phase, spare, :] = jnp.zeros((wide - cu, 4 * cm), BF)

    @pl.loop(0, cu // blk)
    def _(t):
        base = pl.multiple_of(t * blk, blk)
        for c in range(0, cm, 128):
            w = [
                [
                    wup_v[
                        pl.ds(base, blk), (3 * b + e) * cm + c : (3 * b + e) * cm + c + 128
                    ].astype(F32)
                    for e in range(3)
                ]
                for b in range(3)
            ]
            for py in range(2):
                two = [w[0][e] + w[1][e] if py else w[1][e] + w[2][e] for e in range(3)]
                for ro, (e0, e1, e2) in enumerate([two, w[2]] if py else [w[0], two]):
                    for px in range(2):
                        for co, v in enumerate([e0 + e1, e2] if px else [e0, e1 + e2]):
                            at = (2 * ro + co) * cm + c
                            row = pl.multiple_of(base + px * (wide - cu), blk)
                            wc[2 * py + px, pl.ds(row, blk), at : at + 128] = v.astype(BF)

    xs[...] = jnp.zeros_like(xs)
    for k in range(len(steps)):
        @pl.when(there(steps[k]))
        def _():
            copy_to(k, k).wait_recv()

    def image_rows(dr):
        mine = xin[...] if dr == 0 else xrecv[steps.index((dr, 0))]
        left, right = xrecv[steps.index((dr, -1))], xrecv[steps.index((dr, 1))]
        mine, left, right = mine.astype(F32), left.astype(F32), right.astype(F32)
        width = xin.shape[1]
        lane = lax.broadcasted_iota(jnp.int32, mine.shape, 1)
        m = 3 * cl
        whole = jnp.where(
            lane < m,
            pltpu.roll(left, width - (tw - 3) * cl, 1),
            jnp.where(lane < m + tw * cl, pltpu.roll(mine, m, 1), pltpu.roll(right, m + tw * cl, 1)),
        )
        return whole.reshape(frames, th, width)

    xs[2:, off : off + th, :] = image_rows(0)
    if gr > 1:
        xs[2:, 0:3, :] = image_rows(-1)[:, th - 3 :, :]
        xs[2:, off + th : off + th + 3, :] = image_rows(1)[:, 0:3, :]

    fr = frames * rows
    field = xs[...]
    for b in range(3):
        moved = shift_rows(field, b)
        for j in range(nw):
            width = xin.shape[1]
            turned = pltpu.roll(moved, width - j * cl, 2) if j else moved
            for a in range(3):
                g = 3 * a + b
                lhs[j * fr : (j + 1) * fr, g * 128 : (g + 1) * 128] = (
                    turned[a : a + frames, :, :128].reshape(fr, 128).astype(BF)
                )
    hacc[...] = jnp.dot(lhs[...], wpad[...], preferred_element_type=F32)

    def inside(v, j, margin):
        place = col * tw + j - margin
        ok = (place >= 0) & (place < GC * tw)
        if gr > 1:
            row = grow * th + lax.broadcasted_iota(jnp.int32, v.shape, 1) - off
            ok = ok & (row >= 0) & (row < gr * th)
        return jnp.where(ok, v, 0.0)

    kr = keep * rows

    @pl.loop(0, nw)
    def _(j):
        at = pl.multiple_of(j * fr, fr)
        hb = (hacc[pl.ds(at, fr), :] + b_in[...].reshape(1, cm)).astype(BF)
        hbuf[pl.ds(at, fr), :] = hb
        v = hb.astype(F32)
        v = v * lax.rsqrt(jnp.mean(v * v, axis=-1, keepdims=True) + 1e-06) * gain[...].reshape(1, cm)
        half = 0.5 * v
        n = half + half * jnp.tanh(half)
        n = inside(n.reshape(frames, rows, cm), j, 2)
        for b in range(3):
            moved = shift_rows(n, b)
            for a in range(3):
                nab[3 * a + b, pl.ds(pl.multiple_of(j * kr, kr), kr), :] = (
                    moved[a : a + keep].reshape(kr, cm).astype(BF)
                )

    for a in range(3):
        mid_copies[a].wait()
        taps = jnp.concatenate(
            [nab[3 * a + b, e * kr : (e + rw) * kr, :] for b in range(3) for e in range(3)], axis=1
        )
        total = jnp.dot(
            taps, wmid_v[a * part : (a + 1) * part, :], preferred_element_type=F32
        )
        acc[...] = total if a == 0 else acc[...] + total

    @pl.loop(0, rw)
    def _(j):
        at = pl.multiple_of(j * kr, kr)
        own = pl.ds(pl.multiple_of((j + 1) * fr + CACHE * rows, CACHE * rows), kr)
        r = hbuf[own, :].astype(F32) + acc[pl.ds(at, kr), :] + b_mid[...].reshape(1, cm)
        r = inside(r.astype(BF).astype(F32).reshape(keep, rows, cm), j, 1)
        for b in range(3):
            rb[b, pl.ds(at, kr), :] = shift_rows(r, b).reshape(kr, cm).astype(BF)

    strips = 2 * cu // 128
    for py in range(2):
        o = []
        for px in range(2):
            taps = jnp.concatenate(
                [
                    rb[py + ro, (px + co) * kr : (px + co + tw) * kr, :]
                    for ro in range(2)
                    for co in range(2)
                ],
                axis=1,
            )
            o.append(
                lax.dot_general(
                    taps, wc[2 * py + px], (((1,), (1,)), ((), ())), preferred_element_type=F32
                )
            )
        joined = (
            jnp.concatenate([o[0][:, :128], o[0][:, 128:] + o[1][:, :128], o[1][:, 128:]], axis=1)
            + bias3
        )
        for j in range(tw):
            for f in range(keep):
                at = j * kr + f * rows + off
                for c in range(strips):
                    outs[j * strips + c, pl.ds(f * 2 * th + py, th, stride=2), :] = joined[
                        at : at + th, c * 128 : (c + 1) * 128
                    ]
    for f in range(keep):
        for c in range(strips * tw):
            out[f, 0, :, c * 128 : (c + 1) * 128] = outs[c, f * 2 * th : (f + 1) * 2 * th, :].astype(BF)

    for k in range(len(steps)):
        @pl.when(there(steps[k]))
        def _():
            copy_to(k, k).wait_send()


def body(latents, w_in, b_in, gain_mid, w_mid, b_mid, w_up, b_up):
    frames, _, th, packed = latents.shape
    cl = w_in.shape[0] // 27
    tw = packed // cl
    cm, cu = w_in.shape[1], w_up.shape[1]
    gr = lax.axis_size("tile") // GC
    rows, off = (th, 0) if gr == 1 else (2 * th, 3)
    keep = frames - CACHE
    nw, rw = tw + 4, tw + 2
    width = (tw + 6) * cl
    sizes = (frames, th, tw, cl, cm, cu, gr, rows, off)
    near = 2 if gr == 1 else 8
    vm = pl.BlockSpec(memory_space=pltpu.VMEM)
    hbm = pl.BlockSpec(memory_space=pl.ANY)
    flops = 2 * keep * rows * rw * 27 * cm * cm
    return pl.pallas_call(
        functools.partial(kernel, sizes),
        out_shape=jax.ShapeDtypeStruct((keep, 1, 2 * th, 2 * tw * cu), BF),
        in_specs=[vm, hbm, vm, vm, hbm, vm, hbm, vm],
        out_specs=vm,
        scratch_shapes=[
            pltpu.VMEM((frames * th, width), BF),
            pltpu.VMEM((near, frames * th, width), BF),
            pltpu.VMEM((frames + 2, rows, width), F32),
            pltpu.VMEM(w_in.shape, BF),
            pltpu.VMEM((9 * 128, cm), BF),
            pltpu.VMEM(w_mid.shape, BF),
            pltpu.VMEM((cu, 9 * cm), BF),
            pltpu.VMEM((4, 2 * cu - 128, 4 * cm), BF),
            pltpu.VMEM((8, 2 * cu - 128), F32),
            pltpu.VMEM((nw * frames * rows, 9 * 128), BF),
            pltpu.VMEM((nw * frames * rows, cm), F32),
            pltpu.VMEM((nw * frames * rows, cm), BF),
            pltpu.VMEM((9, nw * keep * rows, cm), BF),
            pltpu.VMEM((rw * keep * rows, cm), F32),
            pltpu.VMEM((3, rw * keep * rows, cm), BF),
            pltpu.VMEM((2 * tw * cu // 128, keep * 2 * th, 128), F32),
            pltpu.SemaphoreType.DMA((near,)),
            pltpu.SemaphoreType.DMA((near,)),
            pltpu.SemaphoreType.DMA,
            pltpu.SemaphoreType.DMA,
            pltpu.SemaphoreType.DMA((3,)),
        ],
        compiler_params=pltpu.CompilerParams(
            collective_id=0, has_side_effects=True, vmem_limit_bytes=56 * 2**20
        ),
        cost_estimate=pl.CostEstimate(flops=flops, bytes_accessed=10**7, transcendentals=0),
    )(
        latents.reshape(frames * th, packed),
        w_in,
        b_in,
        gain_mid,
        w_mid,
        b_mid,
        w_up.T,
        b_up,
    )


def solution(mesh):
    placed = (P("clips", "tile", None, None), P(), P(), P(), P(), P(), P(), P())
    return jax.shard_map(
        body, mesh=mesh, in_specs=placed, out_specs=P("clips", "tile", None, None), check_vma=False
    )
```

time: 155 us -> 17.1 us (0.11); the launches traced: 153 us -> 16.9 us
  local copies, waits for them, and re-layouts: 74.2 us -> 1.84 us
  matrix products: 40.2 us -> 0 us
  starting transfers between devices: 17.8 us -> 0 us
  Pallas kernels: 0 us -> 15.1 us
  waiting for transfers between devices: 11.9 us -> 0 us
  other arithmetic: 7.9 us -> 0 us
    reshape x39 -> x0, local copies, waits for them, and re-layouts: 41.9 us -> none  [the longest x27 29.4 us: causal_conv(): window[step_t:step_t + frames]]
    dot_general x53 -> x0, matrix products: 40.2 us -> none  [the longest x25 19.5 us: upsample_conv(): jnp.dot(windows[row_off, col_off], w_up[start:start + mid_chan], preferre...]
    ppermute x12 -> x0, starting transfers between devices: 17.8 us -> none  [passed_along(): return lax.ppermute(block, axis, route)]
    pallas_call x0 -> x1, Pallas kernels: none -> 15.1 us  [body(): pl.pallas_call(functools.partial(kernel, sizes), out_shape=jax.ShapeDtype...]
    ppermute x12 -> x0, waiting for transfers between devices: 11.9 us -> none  [passed_along(): return lax.ppermute(block, axis, route)]
    slice x11 -> x0, local copies, waits for them, and re-layouts: 10 us -> none  [the longest x3 4.97 us: causal_conv(): window[step_t:step_t + frames]]
    unnamed x108 -> x1, local copies, waits for them, and re-layouts: 11.7 us -> 1.84 us
    concatenate x8 -> x0, other arithmetic: 5.63 us -> none  [the longest x5 2.82 us: pad_tile(): return jnp.concatenate([above_part, widened, below_part], axis=1)]
  transfers between devices with their start and end apart: 12 -> 0, of which waited for: 3 -> 0; matrix products, arithmetic and copies ran while one was open for 7% -> 0% of each run, Pallas kernels for 0% -> 0%
where the time goes in v1:
time: 17.1 us; the launch traced here: 16.9 us
  Pallas kernels  15.1 us (88%)
  local copies, waits for them, and re-layouts  1.84 us (11%)
    pallas_call x1, Pallas kernels, body(): pl.pallas_call(functools.partial(kernel, sizes), out_shape=jax.ShapeDtype...  15.1 us
    unnamed x1, local copies, waits for them, and re-layouts  1.84 us

profile of v1, /device:TPU:24, one launch (start us, length us, event | category | flops | bytes accessed | tf_op | source)
XLA Modules:
  0.0 16.9 jit_solution(14882328873449550772)
XLA Ops:
  0.0 15.1 %shard_map.82 = bf16[4,1,16,3840]{3,2,1,0:T(8,128)(2,1)} custom-call(bf16[48,160]{1,0:T(8,128)(2,1)} %bitcast.3, bf16[432,384]{1,0:T(8,128)(2,1)} %w_in.1, f32[384]{0:T(512)} %b_in.1, f32[384]{0:T(512)} %gain.1, bf16[10368,384]{1,0:T(8,128)(2,1)} %w_mid.1, f32[384]{0:T(512)} %b_mid.1, bf16[192,3456]{1,0:T(8,128)(2,1)} %bitcast.2, f32[192]{0:T(256)} %b_up.1), custom_call_target="tpu_custom_call" | custom-call | flops 3057647616 | bytes 10000000 | tf_op jit(solution)/shard_map/pallas_call | solution.py:276
  15.1 1.8 %copy.10 = bf16[4,1,16,3840]{3,2,1,0:T(8,128)(2,1)} copy(bf16[4,1,16,3840]{3,2,1,0:T(8,128)(2,1)} %shard_map.82) | data formatting | bytes 983040

commit v2 on v1

v2 whole, which is shorter than its diff:
```python
import functools

import jax
import jax.numpy as jnp
from jax import lax
from jax.experimental import pallas as pl
from jax.experimental.pallas import tpu as pltpu
from jax.sharding import PartitionSpec as P

CACHE = 2
GC = 16
BF = jnp.bfloat16
F32 = jnp.float32
MESH = pl.DeviceIdType.MESH


def shift_rows(v, b):
    if b == 1:
        return v
    rows = v.shape[1]
    row = lax.broadcasted_iota(jnp.int32, v.shape, 1)
    moved = pltpu.roll(v, 1 if b == 0 else rows - 1, 1)
    return jnp.where(row == (0 if b == 0 else rows - 1), 0.0, moved)


def exchange(sizes, lat, field, xin, xrecv, xs, send_sem, recv_sem):
    frames, th, tw, cl, cm, cu, gr, rows, off = sizes
    me = lax.axis_index("tile")
    col, grow = lax.rem(me, GC), lax.div(me, GC)

    steps = [(0, -1), (0, 1)]
    if gr > 1:
        steps += [(-1, -1), (-1, 0), (-1, 1), (1, -1), (1, 0), (1, 1)]

    def there(step):
        dr, dc = step
        ok = (col + dc >= 0) & (col + dc < GC)
        if dr:
            ok = ok & (grow + dr >= 0) & (grow + dr < gr)
        return ok

    barrier = pltpu.get_barrier_semaphore()
    for step in steps:
        @pl.when(there(step))
        def _():
            pl.semaphore_signal(
                barrier, inc=1, device_id={"tile": me + step[0] * GC + step[1]}, device_id_type=MESH
            )

    xin[...] = jnp.zeros_like(xin)
    xin[:, 0 : tw * cl] = lat[...]
    for k, step in enumerate(steps):
        @pl.when(jnp.logical_not(there(step)))
        def _():
            xrecv[k] = jnp.zeros(xin.shape, BF)

    pl.semaphore_wait(barrier, sum(there(step).astype(jnp.int32) for step in steps))

    def copy_to(k, slot):
        dr, dc = steps[k]
        return pltpu.make_async_remote_copy(
            src_ref=xin,
            dst_ref=xrecv.at[slot],
            send_sem=send_sem.at[k],
            recv_sem=recv_sem.at[slot],
            device_id={"tile": me + dr * GC + dc},
            device_id_type=MESH,
        )

    for k, (dr, dc) in enumerate(steps):
        @pl.when(there((dr, dc)))
        def _():
            copy_to(k, steps.index((-dr, -dc))).start()

    xs[...] = jnp.zeros_like(xs)
    for k in range(len(steps)):
        @pl.when(there(steps[k]))
        def _():
            copy_to(k, k).wait_recv()

    def image_rows(dr):
        mine = xin[...] if dr == 0 else xrecv[steps.index((dr, 0))]
        left, right = xrecv[steps.index((dr, -1))], xrecv[steps.index((dr, 1))]
        mine, left, right = mine.astype(F32), left.astype(F32), right.astype(F32)
        width = xin.shape[1]
        lane = lax.broadcasted_iota(jnp.int32, mine.shape, 1)
        m = 3 * cl
        whole = jnp.where(
            lane < m,
            pltpu.roll(left, width - (tw - 3) * cl, 1),
            jnp.where(lane < m + tw * cl, pltpu.roll(mine, m, 1), pltpu.roll(right, m + tw * cl, 1)),
        )
        return whole.reshape(frames, th, width)

    xs[:, off : off + th, :] = image_rows(0)
    if gr > 1:
        xs[:, 0:3, :] = image_rows(-1)[:, th - 3 :, :]
        xs[:, off + th : off + th + 3, :] = image_rows(1)[:, 0:3, :]

    field[...] = xs[...].reshape(field.shape).astype(BF)

    for k in range(len(steps)):
        @pl.when(there(steps[k]))
        def _():
            copy_to(k, k).wait_send()


def convolve(
    sizes, field, w_in, b_in, gain, w_mid, b_mid, w_up, b_up, out,
    win_v, wpad, wmid_v, wup_v, wc, bias, lhs, hacc, hbuf, nab, acc, rb, outs,
    in_sem, up_sem, mid_sem,
):
    frames, th, tw, cl, cm, cu, gr, rows, off = sizes
    keep = frames - CACHE
    nw, rw = tw + 4, tw + 2
    width = (tw + 6) * cl
    me = lax.axis_index("tile")
    col, grow = lax.rem(me, GC), lax.div(me, GC)

    in_copy = pltpu.make_async_copy(w_in, win_v, in_sem)
    up_copy = pltpu.make_async_copy(w_up, wup_v, up_sem)
    mid_copy = pltpu.make_async_copy(w_mid, wmid_v, mid_sem)

    in_copy.start()
    mid_copy.start()
    up_copy.start()

    fr = frames * rows
    image = jnp.concatenate(
        [jnp.zeros((2, rows, width), F32), field[...].astype(F32).reshape(frames, rows, width)], axis=0
    )
    for b in range(3):
        moved = shift_rows(image, b)
        for j in range(nw):
            turned = pltpu.roll(moved, width - j * cl, 2) if j else moved
            for a in range(3):
                g = 3 * a + b
                lhs[j * fr : (j + 1) * fr, g * 128 : (g + 1) * 128] = (
                    turned[a : a + frames, :, :128].reshape(fr, 128).astype(BF)
                )
    wpad[...] = jnp.zeros_like(wpad)
    in_copy.wait()
    for g in range(9):
        wpad[g * 128 : g * 128 + 3 * cl, :] = win_v[g * 3 * cl : (g + 1) * 3 * cl, :]

    hacc[...] = jnp.dot(lhs[...], wpad[...], preferred_element_type=F32)

    wide = 2 * cu - 128
    bias[...] = jnp.zeros_like(bias)
    bias[0:1, 0:cu] = b_up[...].reshape(1, cu)
    first = bias[...]
    second = pltpu.roll(first, wide - cu, 1)
    bias3 = jnp.concatenate(
        [first[0:1, :128], first[0:1, 128:] + second[0:1, :128], second[0:1, 128:]], axis=1
    )

    def inside(v, j, margin):
        place = col * tw + j - margin
        ok = (place >= 0) & (place < GC * tw)
        if gr > 1:
            row = grow * th + lax.broadcasted_iota(jnp.int32, v.shape, 1) - off
            ok = ok & (row >= 0) & (row < gr * th)
        return jnp.where(ok, v, 0.0)

    kr = keep * rows

    @pl.loop(0, nw, unroll=nw)
    def _(j):
        at = pl.multiple_of(j * fr, fr)
        hb = (hacc[pl.ds(at, fr), :] + b_in[...].reshape(1, cm)).astype(BF)
        hbuf[pl.ds(at, fr), :] = hb
        v = hb.astype(F32)
        v = v * lax.rsqrt(jnp.mean(v * v, axis=-1, keepdims=True) + 1e-06) * gain[...].reshape(1, cm)
        half = 0.5 * v
        n = half + half * jnp.tanh(half)
        n = inside(n.reshape(frames, rows, cm), j, 2)
        for b in range(3):
            moved = shift_rows(n, b)
            for a in range(3):
                nab[3 * a + b, pl.ds(pl.multiple_of(j * kr, kr), kr), :] = (
                    moved[a : a + keep].reshape(kr, cm).astype(BF)
                )

    up_copy.wait()
    blk = 16
    for phase in range(4):
        spare = pl.ds(0, wide - cu) if phase % 2 else pl.ds(cu, wide - cu)
        wc[phase, spare, :] = jnp.zeros((wide - cu, 4 * cm), BF)

    @pl.loop(0, cu // blk)
    def _(t):
        base = pl.multiple_of(t * blk, blk)
        for c in range(0, cm, 128):
            w = [
                [
                    wup_v[
                        pl.ds(base, blk), (3 * b + e) * cm + c : (3 * b + e) * cm + c + 128
                    ].astype(F32)
                    for e in range(3)
                ]
                for b in range(3)
            ]
            for py in range(2):
                two = [w[0][e] + w[1][e] if py else w[1][e] + w[2][e] for e in range(3)]
                for ro, (e0, e1, e2) in enumerate([two, w[2]] if py else [w[0], two]):
                    for px in range(2):
                        for co, v in enumerate([e0 + e1, e2] if px else [e0, e1 + e2]):
                            at = (2 * ro + co) * cm + c
                            row = pl.multiple_of(base + px * (wide - cu), blk)
                            wc[2 * py + px, pl.ds(row, blk), at : at + 128] = v.astype(BF)

    mid_copy.wait()
    taps = jnp.concatenate(
        [nab[i, e * kr : (e + rw) * kr, :] for i in range(9) for e in range(3)], axis=1
    )
    acc[...] = jnp.dot(taps, wmid_v[...], preferred_element_type=F32)

    @pl.loop(0, rw, unroll=rw)
    def _(j):
        at = pl.multiple_of(j * kr, kr)
        own = pl.ds(pl.multiple_of((j + 1) * fr + CACHE * rows, CACHE * rows), kr)
        r = hbuf[own, :].astype(F32) + acc[pl.ds(at, kr), :] + b_mid[...].reshape(1, cm)
        r = inside(r.astype(BF).astype(F32).reshape(keep, rows, cm), j, 1)
        for b in range(3):
            rb[b, pl.ds(at, kr), :] = shift_rows(r, b).reshape(kr, cm).astype(BF)

    strips = 2 * cu // 128
    for py in range(2):
        o = []
        for px in range(2):
            taps = jnp.concatenate(
                [
                    rb[py + ro, (px + co) * kr : (px + co + tw) * kr, :]
                    for ro in range(2)
                    for co in range(2)
                ],
                axis=1,
            )
            o.append(
                lax.dot_general(
                    taps, wc[2 * py + px], (((1,), (1,)), ((), ())), preferred_element_type=F32
                )
            )
        joined = (
            jnp.concatenate([o[0][:, :128], o[0][:, 128:] + o[1][:, :128], o[1][:, 128:]], axis=1)
            + bias3
        )
        for j in range(tw):
            for f in range(keep):
                at = j * kr + f * rows + off
                for c in range(strips):
                    outs[j * strips + c, pl.ds(f * 2 * th + py, th, stride=2), :] = joined[
                        at : at + th, c * 128 : (c + 1) * 128
                    ]
    for f in range(keep):
        for c in range(strips * tw):
            out[f, 0, :, c * 128 : (c + 1) * 128] = outs[c, f * 2 * th : (f + 1) * 2 * th, :].astype(BF)


def body(latents, w_in, b_in, gain_mid, w_mid, b_mid, w_up, b_up):
    frames, _, th, packed = latents.shape
    cl = w_in.shape[0] // 27
    tw = packed // cl
    cm, cu = w_in.shape[1], w_up.shape[1]
    gr = lax.axis_size("tile") // GC
    rows, off = (th, 0) if gr == 1 else (2 * th, 3)
    keep = frames - CACHE
    nw, rw = tw + 4, tw + 2
    width = (tw + 6) * cl
    sizes = (frames, th, tw, cl, cm, cu, gr, rows, off)
    near = 2 if gr == 1 else 8
    vm = pl.BlockSpec(memory_space=pltpu.VMEM)
    hbm = pl.BlockSpec(memory_space=pl.ANY)
    field = pl.pallas_call(
        functools.partial(exchange, sizes),
        out_shape=jax.ShapeDtypeStruct((frames * rows, width), BF),
        in_specs=[vm],
        out_specs=vm,
        scratch_shapes=[
            pltpu.VMEM((frames * th, width), BF),
            pltpu.VMEM((near, frames * th, width), BF),
            pltpu.VMEM((frames, rows, width), F32),
            pltpu.SemaphoreType.DMA((near,)),
            pltpu.SemaphoreType.DMA((near,)),
        ],
        compiler_params=pltpu.CompilerParams(
            collective_id=0, has_side_effects=True, vmem_limit_bytes=4 * 2**20
        ),
        cost_estimate=pl.CostEstimate(flops=10**6, bytes_accessed=10**5, transcendentals=0),
    )(latents.reshape(frames * th, packed))
    flops = 2 * keep * rows * rw * 27 * cm * cm
    return pl.pallas_call(
        functools.partial(convolve, sizes),
        out_shape=jax.ShapeDtypeStruct((keep, 1, 2 * th, 2 * tw * cu), BF),
        in_specs=[vm, hbm, vm, vm, hbm, vm, hbm, vm],
        out_specs=vm,
        scratch_shapes=[
            pltpu.VMEM(w_in.shape, BF),
            pltpu.VMEM((9 * 128, cm), BF),
            pltpu.VMEM(w_mid.shape, BF),
            pltpu.VMEM((cu, 9 * cm), BF),
            pltpu.VMEM((4, 2 * cu - 128, 4 * cm), BF),
            pltpu.VMEM((8, 2 * cu - 128), F32),
            pltpu.VMEM((nw * frames * rows, 9 * 128), BF),
            pltpu.VMEM((nw * frames * rows, cm), F32),
            pltpu.VMEM((nw * frames * rows, cm), BF),
            pltpu.VMEM((9, nw * keep * rows, cm), BF),
            pltpu.VMEM((rw * keep * rows, cm), F32),
            pltpu.VMEM((3, rw * keep * rows, cm), BF),
            pltpu.VMEM((2 * tw * cu // 128, keep * 2 * th, 128), F32),
            pltpu.SemaphoreType.DMA,
            pltpu.SemaphoreType.DMA,
            pltpu.SemaphoreType.DMA,
        ],
        compiler_params=pltpu.CompilerParams(vmem_limit_bytes=40 * 2**20),
        cost_estimate=pl.CostEstimate(flops=flops, bytes_accessed=10**7, transcendentals=0),
    )(field, w_in, b_in, gain_mid, w_mid, b_mid, w_up.T, b_up)


def solution(mesh):
    placed = (P("clips", "tile", None, None), P(), P(), P(), P(), P(), P(), P())
    return jax.shard_map(
        body, mesh=mesh, in_specs=placed, out_specs=P("clips", "tile", None, None), check_vma=False
    )
```

time: 17.1 us -> 23.3 us (1.36)
  local copies, waits for them, and re-layouts: 1.84 us -> 9.01 us
  Pallas kernels: 15.1 us -> 13.9 us
    unnamed x1 -> x16, local copies, waits for them, and re-layouts: 1.84 us -> 9.01 us
    pallas_call x1 -> x2, Pallas kernels: 15.1 us -> 13.9 us  [the longest x1 9.64 us: body(): pl.pallas_call(functools.partial(convolve, sizes), out_shape=jax.ShapeDty...]
where the time goes in v2:
time: 23.3 us; the launch traced here: 23 us
  Pallas kernels  13.9 us (60%)
  local copies, waits for them, and re-layouts  9.01 us (39%)
    pallas_call x1, Pallas kernels, body(): pl.pallas_call(functools.partial(convolve, sizes), out_shape=jax.ShapeDty...  9.64 us
    unnamed x16, local copies, waits for them, and re-layouts  9.01 us
    pallas_call x1, Pallas kernels, body(): pl.pallas_call(functools.partial(exchange, sizes), out_shape=jax.ShapeDty...  4.28 us

profile of v2, /device:TPU:24, one launch (start us, length us, event | category | flops | bytes accessed | tf_op | source)
XLA Modules:
  0.0 23.0 jit_solution(16392372847181793820)
XLA Ops:
  0.0 0.0 copy-start
  0.0 0.7 %copy-done = bf16[6,1,8,160]{3,2,1,0:T(8,128)(2,1)S(1)} copy-done((bf16[6,1,8,160]{3,2,1,0:T(8,128)(2,1)S(1)}, bf16[6,1,8,160]{3,2,1,0:T(8,128)(2,1)}, u32[]{:S(2)}) %copy-start) | copy-done | bytes 15384
  0.7 4.3 %shard_map.82.field = bf16[48,256]{1,0:T(8,128)(2,1)S(1)} custom-call(bf16[48,160]{1,0:T(8,128)(2,1)S(1)} %bitcast.2), custom_call_target="tpu_custom_call" | custom-call | flops 1000000 | bytes 100000 | tf_op jit(solution)/shard_map/pallas_call | solution.py:274
  5.0 0.0 copy-start.1
  5.0 3.3 %copy-done.1 = bf16[10368,384]{1,0:T(8,128)(2,1)S(1)} copy-done((bf16[10368,384]{1,0:T(8,128)(2,1)S(1)}, bf16[10368,384]{1,0:T(8,128)(2,1)}, u32[]{:S(2)}) %copy-start.1) | copy-done | bytes 7962648
  8.3 0.0 copy-start.2
  8.3 1.3 %copy-done.2 = bf16[3456,192]{0,1:T(8,128)(2,1)S(1)} copy-done((bf16[3456,192]{0,1:T(8,128)(2,1)S(1)}, bf16[3456,192]{0,1:T(8,128)(2,1)}, u32[]{:S(2)}) %copy-start.2) | copy-done | bytes 1327128
  9.6 0.0 copy-start.3
  9.6 1.0 %copy-done.3 = bf16[432,384]{1,0:T(8,128)(2,1)S(1)} copy-done((bf16[432,384]{1,0:T(8,128)(2,1)S(1)}, bf16[432,384]{1,0:T(8,128)(2,1)}, u32[]{:S(2)}) %copy-start.3) | copy-done | bytes 331800
  10.6 0.0 copy-start.4
  10.6 0.7 %copy-done.4 = f32[384]{0:T(512)S(1)} copy-done((f32[384]{0:T(512)S(1)}, f32[384]{0:T(512)}, u32[]{:S(2)}) %copy-start.4) | copy-done | bytes 1560
  11.3 0.0 copy-start.5
  11.3 0.7 %copy-done.5 = f32[384]{0:T(512)S(1)} copy-done((f32[384]{0:T(512)S(1)}, f32[384]{0:T(512)}, u32[]{:S(2)}) %copy-start.5) | copy-done | bytes 1560
  12.0 0.0 copy-start.6
  12.0 0.7 %copy-done.6 = f32[384]{0:T(512)S(1)} copy-done((f32[384]{0:T(512)S(1)}, f32[384]{0:T(512)}, u32[]{:S(2)}) %copy-start.6) | copy-done | bytes 1560
  12.6 0.0 copy-start.7
  12.6 0.7 %copy-done.7 = f32[192]{0:T(256)S(1)} copy-done((f32[192]{0:T(256)S(1)}, f32[192]{0:T(256)}, u32[]{:S(2)}) %copy-start.7) | copy-done | bytes 792
  13.3 9.6 %shard_map.83 = bf16[4,1,16,3840]{3,2,1,0:T(8,128)(2,1)} custom-call(bf16[48,256]{1,0:T(8,128)(2,1)S(1)} %shard_map.82.field, bf16[432,384]{1,0:T(8,128)(2,1)S(1)} %copy-done.3, f32[384]{0:T(512)S(1)} %copy-done.4, f32[384]{0:T(512)S(1)} %copy-done.5, bf16[10368,384]{1,0:T(8,128)(2,1)S(1)} %copy-done.1, f32[384]{0:T(512)S(1)} %copy-done.6, ...), custom_call_target="tpu_custom_call" | custom-call | flops 3057647616 | bytes 10000000 | tf_op jit(solution)/shard_map/pallas_call | solution.py:292
Async XLA Ops:
  0.0 0.7 %copy-start = (bf16[6,1,8,160]{3,2,1,0:T(8,128)(2,1)S(1)}, bf16[6,1,8,160]{3,2,1,0:T(8,128)(2,1)}, u32[]{:S(2)}) copy-start(bf16[6,1,8,160]{3,2,1,0:T(8,128)(2,1)} %param.8) | copy-start | bytes 46084
  5.0 3.3 %copy-start.1 = (bf16[10368,384]{1,0:T(8,128)(2,1)S(1)}, bf16[10368,384]{1,0:T(8,128)(2,1)}, u32[]{:S(2)}) copy-start(bf16[10368,384]{1,0:T(8,128)(2,1)} %w_mid.1) | copy-start | bytes 23887876
  8.3 1.3 %copy-start.2 = (bf16[3456,192]{0,1:T(8,128)(2,1)S(1)}, bf16[3456,192]{0,1:T(8,128)(2,1)}, u32[]{:S(2)}) copy-start(bf16[3456,192]{0,1:T(8,128)(2,1)} %param.14) | copy-start | bytes 3981316
  9.6 1.0 %copy-start.3 = (bf16[432,384]{1,0:T(8,128)(2,1)S(1)}, bf16[432,384]{1,0:T(8,128)(2,1)}, u32[]{:S(2)}) copy-start(bf16[432,384]{1,0:T(8,128)(2,1)} %w_in.1) | copy-start | bytes 995332
  10.6 0.7 %copy-start.4 = (f32[384]{0:T(512)S(1)}, f32[384]{0:T(512)}, u32[]{:S(2)}) copy-start(f32[384]{0:T(512)} %b_in.1) | copy-start | bytes 4612
  11.3 0.7 %copy-start.5 = (f32[384]{0:T(512)S(1)}, f32[384]{0:T(512)}, u32[]{:S(2)}) copy-start(f32[384]{0:T(512)} %gain.1) | copy-start | bytes 4612
  12.0 0.7 %copy-start.6 = (f32[384]{0:T(512)S(1)}, f32[384]{0:T(512)}, u32[]{:S(2)}) copy-start(f32[384]{0:T(512)} %b_mid.1) | copy-start | bytes 4612
  12.6 0.7 %copy-start.7 = (f32[192]{0:T(256)S(1)}, f32[192]{0:T(256)}, u32[]{:S(2)}) copy-start(f32[192]{0:T(256)} %b_up.1) | copy-start | bytes 2308

commit v3 on v1

--- a/solution.py
+++ b/solution.py
@@ -36,13 +36,7 @@
 
     in_copy = pltpu.make_async_copy(w_in, win_v, in_sem)
     up_copy = pltpu.make_async_copy(w_up, wup_v, up_sem)
-    part = 9 * cm
-    mid_copies = [
-        pltpu.make_async_copy(
-            w_mid.at[pl.ds(a * part, part), :], wmid_v.at[pl.ds(a * part, part), :], mid_sem.at[a]
-        )
-        for a in range(3)
-    ]
+    mid_copy = pltpu.make_async_copy(w_mid, wmid_v, mid_sem)
 
     steps = [(0, -1), (0, 1)]
     if gr > 1:
@@ -65,8 +59,7 @@
 
     in_copy.start()
     up_copy.start()
-    for copy in mid_copies:
-        copy.start()
+    mid_copy.start()
 
     xin[...] = jnp.zeros_like(xin)
     xin[:, 0 : tw * cl] = lat[...]
@@ -184,7 +177,7 @@
 
     kr = keep * rows
 
-    @pl.loop(0, nw)
+    @pl.loop(0, nw, unroll=nw)
     def _(j):
         at = pl.multiple_of(j * fr, fr)
         hb = (hacc[pl.ds(at, fr), :] + b_in[...].reshape(1, cm)).astype(BF)
@@ -201,17 +194,13 @@
                     moved[a : a + keep].reshape(kr, cm).astype(BF)
                 )
 
-    for a in range(3):
-        mid_copies[a].wait()
-        taps = jnp.concatenate(
-            [nab[3 * a + b, e * kr : (e + rw) * kr, :] for b in range(3) for e in range(3)], axis=1
-        )
-        total = jnp.dot(
-            taps, wmid_v[a * part : (a + 1) * part, :], preferred_element_type=F32
-        )
-        acc[...] = total if a == 0 else acc[...] + total
-
-    @pl.loop(0, rw)
+    mid_copy.wait()
+    taps = jnp.concatenate(
+        [nab[i, e * kr : (e + rw) * kr, :] for i in range(9) for e in range(3)], axis=1
+    )
+    acc[...] = jnp.dot(taps, wmid_v[...], preferred_element_type=F32)
+
+    @pl.loop(0, rw, unroll=rw)
     def _(j):
         at = pl.multiple_of(j * kr, kr)
         own = pl.ds(pl.multiple_of((j + 1) * fr + CACHE * rows, CACHE * rows), kr)
@@ -299,7 +288,7 @@
             pltpu.SemaphoreType.DMA((near,)),
             pltpu.SemaphoreType.DMA,
             pltpu.SemaphoreType.DMA,
-            pltpu.SemaphoreType.DMA((3,)),
+            pltpu.SemaphoreType.DMA,
         ],
         compiler_params=pltpu.CompilerParams(
             collective_id=0, has_side_effects=True, vmem_limit_bytes=56 * 2**20

time: 17.1 us -> 15.1 us (0.88)
  Pallas kernels: 15.1 us -> 13.1 us
    pallas_call x1, Pallas kernels: 15.1 us -> 13.1 us  [body(): pl.pallas_call(functools.partial(kernel, sizes), out_shape=jax.ShapeDtype...]
where the time goes in v3:
time: 15.1 us; the launch traced here: 14.9 us
  Pallas kernels  13.1 us (87%)
  local copies, waits for them, and re-layouts  1.84 us (12%)
    pallas_call x1, Pallas kernels, body(): pl.pallas_call(functools.partial(kernel, sizes), out_shape=jax.ShapeDtype...  13.1 us
    unnamed x1, local copies, waits for them, and re-layouts  1.84 us

profile of v3, /device:TPU:24, one launch (start us, length us, event | category | flops | bytes accessed | tf_op | source)
XLA Modules:
  0.0 14.9 jit_solution(6286562839587308778)
XLA Ops:
  0.0 13.1 %shard_map.82 = bf16[4,1,16,3840]{3,2,1,0:T(8,128)(2,1)} custom-call(bf16[48,160]{1,0:T(8,128)(2,1)} %bitcast.3, bf16[432,384]{1,0:T(8,128)(2,1)} %w_in.1, f32[384]{0:T(512)} %b_in.1, f32[384]{0:T(512)} %gain.1, bf16[10368,384]{1,0:T(8,128)(2,1)} %w_mid.1, f32[384]{0:T(512)} %b_mid.1, bf16[192,3456]{1,0:T(8,128)(2,1)} %bitcast.2, f32[192]{0:T(256)} %b_up.1), custom_call_target="tpu_custom_call" | custom-call | flops 3057647616 | bytes 10000000 | tf_op jit(solution)/shard_map/pallas_call | solution.py:265
  13.1 1.8 %copy.10 = bf16[4,1,16,3840]{3,2,1,0:T(8,128)(2,1)} copy(bf16[4,1,16,3840]{3,2,1,0:T(8,128)(2,1)} %shard_map.82) | data formatting | bytes 983040
